TPU v7x, 128 devices: a whole 4x4x4 slice. The times are simulated.
128 devices in a mesh: row: 8 (over y, x_hi), col: 16 (over x_lo, z, core).
Axes of the slice: x: 4 (x_hi: 2, x_lo: 2; x = x_hi * 2 + x_lo), y: 4, z: 4, core: 2. Of those that a mesh axis runs over, the one named last changes fastest.
Arguments:
- a_blocks: float32 [8, 16, 4, 128, 128], P('row', 'col'), may hold values from -1.2 to 1.2
- a_index: int32 [8, 16, 4], P('row', 'col'), may hold values from -1 to 63, as said below
- b_blocks: float32 [8, 16, 2, 8, 128, 128], P('row', 'col'), may hold values from -1.2 to 1.2
- b_index: int32 [8, 16, 2, 8], P('row', 'col'), may hold values from -1 to 63, as said below
- c_index: int32 [8, 16, 16], P('row', 'col'), may hold values from -1 to 63, as said below
Outputs:
- c_blocks: float32 [8, 16, 16, 128, 128], P('row', 'col')
Inputs may be any that keep to these rules, and one draw needn't show every extreme that they name: `a_index`: within each tile the non-negative entries are distinct and come before the entries -1, which mark empty slots; every tile has at least one block and some tile has all 4 slots filled. `b_index`: within each panel of a device the non-negative entries are distinct and come before the entries -1, which mark empty slots; every panel has at least one block and some panel has all 8 slots filled. `c_index`: within each tile the non-negative entries are distinct and come before the entries -1, which mark empty slots; every tile keeps at least one block and some tile has all 16 slots filled.
All inputs are finite; a program needn't handle non-finite values.
Results may differ from a plain program's by a relative error of at most 0.0003.
Values sent between devices are 32-bit elements; how exact they have to be, the bound alone decides.
No kernel may reach another device: no remote copies, remote signals or barrier semaphores. Data moves between devices by JAX's collectives and lax.ppermute only.
A program may use at most 192 MiB of HBM per device.

v0:
```python
import functools

import jax
import jax.numpy as jnp
from jax import lax
from jax.experimental import pallas as pl
from jax.experimental.pallas import tpu as pltpu
from jax.sharding import PartitionSpec as P

PK = 8
NBD = 8
CAP = 6
AHEAD = 4


def targets(a_where, b_where):
    meet = (a_where >= 0) & (b_where >= 0) & (a_where % PK == b_where // NBD)
    return jnp.where(meet, (a_where // PK) * NBD + b_where % NBD, -2)


def pack_kernel(order_ref, count_ref, blocks_ref, *rest):
    outs, sems = rest[:2], rest[2]

    def each(act):
        for half in range(2):
            for e in range(CAP):

                @pl.when(e < count_ref[half])
                def _():
                    act(
                        pltpu.make_async_copy(
                            blocks_ref.at[order_ref[half, e]],
                            outs[half].at[e],
                            sems.at[half, e],
                        )
                    )

    each(lambda copy: copy.start())
    each(lambda copy: copy.wait())


def pack(order, count, blocks):
    whole = pl.BlockSpec((CAP,) + blocks.shape[1:], lambda i, *_: (0, 0, 0))
    return pl.pallas_call(
        pack_kernel,
        grid_spec=pltpu.PrefetchScalarGridSpec(
            num_scalar_prefetch=2,
            grid=(1,),
            in_specs=[pl.BlockSpec(memory_space=pl.ANY)],
            out_specs=[whole] * 2,
            scratch_shapes=[pltpu.SemaphoreType.DMA((2, CAP))],
        ),
        out_shape=[jax.ShapeDtypeStruct((CAP,) + blocks.shape[1:], blocks.dtype)] * 2,
        compiler_params=pltpu.CompilerParams(vmem_limit_bytes=48 << 20),
        name="pack",
    )(order, count, blocks)


def product_kernel(first, parts, a_at, b_part, b_at, c_at, count_ref, a_ref, *rest):
    b_refs, rest = rest[:parts], rest[parts:]
    if first:
        out_ref, a_buf, b_buf, a_sem, b_sem = rest
    else:
        sum_ref, out_ref, a_buf, b_buf, a_sem, b_sem = rest

    def a_copy(n):
        slot = n % AHEAD
        return pltpu.make_async_copy(a_ref.at[a_at[n]], a_buf.at[slot], a_sem.at[slot])

    def b_copy(n, part):
        slot = n % AHEAD
        return pltpu.make_async_copy(b_refs[part].at[b_at[n]], b_buf.at[slot], b_sem.at[slot])

    def fetch(n):
        a_copy(n).start()
        for part in range(parts):

            @pl.when(b_part[n] == part)
            def _():
                b_copy(n, part).start()

    count = count_ref[0]
    for n in range(AHEAD):

        @pl.when(n < count)
        def _():
            fetch(n)

    if first:
        out_ref[...] = jnp.zeros_like(out_ref)
    else:
        out_ref[...] = sum_ref[...]

    def step(n, carry):
        a_copy(n).wait()
        b_copy(n, 0).wait()
        slot = n % AHEAD
        out_ref[c_at[n]] += jnp.dot(
            a_buf[slot],
            b_buf[slot],
            precision=lax.Precision.HIGHEST,
            preferred_element_type=jnp.float32,
        )

        @pl.when(n + AHEAD < count)
        def _():
            fetch(n + AHEAD)

        return carry

    lax.fori_loop(0, count, step, 0)


def products(lists, count, a_all, b_parts, total, slots):
    first = total is None
    size = a_all.shape[-1]
    whole = pl.BlockSpec((slots, size, size), lambda i, *_: (0, 0, 0))
    anywhere = pl.BlockSpec(memory_space=pl.ANY)
    return pl.pallas_call(
        functools.partial(product_kernel, first, len(b_parts)),
        grid_spec=pltpu.PrefetchScalarGridSpec(
            num_scalar_prefetch=5,
            grid=(1,),
            in_specs=[anywhere] * (1 + len(b_parts)) + ([] if first else [whole]),
            out_specs=whole,
            scratch_shapes=[
                pltpu.VMEM((AHEAD, size, size), jnp.float32),
                pltpu.VMEM((AHEAD, size, size), jnp.float32),
                pltpu.SemaphoreType.DMA((AHEAD,)),
                pltpu.SemaphoreType.DMA((AHEAD,)),
            ],
        ),
        out_shape=jax.ShapeDtypeStruct((slots, size, size), jnp.float32),
        compiler_params=pltpu.CompilerParams(vmem_limit_bytes=48 << 20),
        name="products",
    )(*lists, count, a_all, *b_parts, *([] if first else [total]))


def before(flags):
    n = flags.shape[0]
    earlier = jnp.arange(n)[None, :] < jnp.arange(n)[:, None]
    return jnp.sum(jnp.where(earlier & flags[None, :], 1, 0), axis=1, dtype=jnp.int32)


def listed(flags, place, values, length):
    hit = flags[None, :] & (place[None, :] == jnp.arange(length)[:, None])
    return [jnp.sum(jnp.where(hit, v[None, :], 0), axis=1, dtype=jnp.int32) for v in values]


def ring(block, rows, step):
    return lax.ppermute(block, "row", [((i + 2 * step) % rows, i) for i in range(rows)])


def around(block, rows):
    behind, ahead = ring(block, rows, -1), ring(block, rows, 1)
    far = (ring(behind[: CAP // 2], rows, -1), ring(ahead[CAP // 2 :], rows, 1))
    return [block, behind, ahead, *far]


def per_device(a_blocks, a_index, b_blocks, b_index, c_index):
    rows = lax.axis_size("row")
    columns = lax.axis_size("col")
    row = lax.axis_index("row")
    column = lax.axis_index("col")
    hold = columns // rows
    sa, sb, sc = a_blocks.shape[2], b_blocks.shape[3], c_index.shape[2]
    held = hold * sb
    size = a_blocks.shape[-1]
    half = row % 2

    mine = jnp.concatenate([a_index[0, 0], b_index[0, 0].reshape(-1), c_index[0, 0]])
    mine = jnp.pad(mine, (0, 128 - mine.shape[0]))[None]
    spots = lax.all_gather(mine, ("row", "col"), tiled=True).reshape(rows, columns, -1)
    a_all = lax.all_gather(a_blocks[0, 0], "col").reshape(columns * sa, size, size)
    a_where = spots[:, :, :sa]
    b_where = spots[:, :, sa : sa + held]
    c_where = spots[:, :, sa + held : sa + held + sc]

    a_wide = jnp.repeat(a_where.transpose(0, 2, 1), sb, axis=2)
    b_wide = b_where.transpose(1, 0, 2).reshape(columns, rows * held)

    def needed(b_line, c_column):
        lands = targets(a_wide, b_line[None, None, :])
        kept = lands[:, :, None, :] == c_column[:, None, :, None]
        kept = kept.reshape(rows // 2, 2, sa, sc, rows * held)
        return jnp.any(kept, axis=(0, 2, 3)).reshape(2, rows, held)

    b_mine = lax.dynamic_index_in_dim(b_wide, column, 0, keepdims=False)
    c_mine = lax.dynamic_index_in_dim(c_where, column, 1, keepdims=False)
    need = needed(b_mine, c_mine)
    earlier = jnp.arange(held)[None, :] < jnp.arange(held)[:, None]
    place = jnp.sum(
        jnp.where(earlier & need[:, :, None, :], 1, 0), axis=3, dtype=jnp.int32
    )

    own_need = lax.dynamic_index_in_dim(need, row, 1, keepdims=False)
    own_place = lax.dynamic_index_in_dim(place, row, 1, keepdims=False)
    own_count = jnp.sum(own_need, axis=1, dtype=jnp.int32)

    a_row = lax.dynamic_index_in_dim(a_wide, row, 0, keepdims=False)
    lands = targets(a_row, b_mine[None, :])
    hits = lands[:, None, :] == c_index[0, 0][None, :, None]
    live = jnp.any(hits, axis=1).reshape(-1)
    c_slot = jnp.sum(
        jnp.where(hits, jnp.arange(sc)[None, :, None], 0), axis=1, dtype=jnp.int32
    ).reshape(-1)
    line = jnp.arange(columns * sb)
    a_slot = ((line // sb)[None, :] * sa + jnp.arange(sa)[:, None]).reshape(-1)
    owner = line // held
    across = owner % 2 != half
    steps = (owner // 2 - row // 2) % (rows // 2)
    b_ring = jnp.select([steps == 0, steps == 3, steps == 1], [0, 1, 2], 3)
    b_place = lax.dynamic_index_in_dim(place, half, 0, keepdims=False).reshape(-1)

    def for_all(values):
        return jnp.broadcast_to(values[None, :], (sa, columns * sb)).reshape(-1)

    counts = jnp.sum(jax.vmap(needed, in_axes=(0, 1))(b_wide, c_where), axis=3, dtype=jnp.int32)
    most = jnp.max(counts)

    b_held = b_blocks[0, 0].reshape(held, size, size)

    def one_round(turn, total):
        base = turn * CAP
        orders = [
            listed(own_need[h], own_place[h] - base, [jnp.arange(held)], CAP)[0]
            for h in range(2)
        ]
        orders = jnp.stack(orders)
        amounts = jnp.clip(own_count - base, 0, CAP)
        keep = lax.dynamic_index_in_dim(orders, half, 0)
        give = lax.dynamic_index_in_dim(orders, 1 - half, 0)
        amounts = jnp.stack([amounts[half], amounts[1 - half]])
        here, there = pack(jnp.concatenate([keep, give]), amounts, b_held)
        crossed = lax.ppermute(there, "row", [(i ^ 1, i) for i in range(rows)])
        parts = around(here, rows) + around(crossed, rows)

        spot = b_place - base
        late = (b_ring == 3) & (spot >= CAP // 2)
        part = b_ring + jnp.where(late, 1, 0) + jnp.where(across, 5, 0)
        spot_in = spot - jnp.where(late, CAP // 2, 0)
        now = live & for_all((spot >= 0) & (spot < CAP))
        lists = listed(
            now,
            before(now),
            [a_slot, for_all(part), for_all(spot_in), c_slot],
            now.shape[0],
        )
        return products(lists, jnp.sum(now, dtype=jnp.int32)[None], a_all, parts, total, sc)

    total = one_round(0, None)
    rounds = (most + CAP - 1) // CAP
    _, total = lax.while_loop(
        lambda state: state[0] < rounds,
        lambda state: (state[0] + 1, one_round(state[0], state[1])),
        (jnp.int32(1), total),
    )
    return total[None, None]


def solution(mesh):
    in_specs = (
        P("row", "col", None, None, None),
        P("row", "col", None),
        P("row", "col", None, None, None, None),
        P("row", "col", None, None),
        P("row", "col", None),
    )
    out_specs = P("row", "col", None, None, None)
    return jax.shard_map(
        per_device, mesh=mesh, in_specs=in_specs, out_specs=out_specs, check_vma=False
    )
```

profile of v0, /device:TPU:4, one launch (start us, length us, event | category | flops | bytes accessed | tf_op | source)
XLA Modules:
  0.0 95.5 jit_solution(17117057733009830028)
XLA Ops:
  6.5 0.0 all-gather.5.cloned.1.call-start
  6.5 0.7 all-gather.5.cloned.1.call-update
  7.3 0.8 reshape_squeeze.6
  8.0 0.7 pad_add_fusion.5
  8.8 32.2 %all-gather.2 = s32[128,1,128]{2,1,0:T(1,128)S(1)} all-gather(s32[1,1,128]{2,1,0:T(1,128)S(1)} %pad_bitcast_fusion), channel_id=2, replica_groups=mesh['row'=8,'col'=16] {'row','col'}, dimensions={0}, use_global_device_ids=true | all-gather | bytes 66048 | tf_op jit(solution)/shard_map/all_gather | solution.py:173
  41.0 0.1 copy.27
  41.2 0.1 fusion.39
  41.3 0.1 reshape.706
  41.4 0.1 broadcast_in_dim.307
  41.5 0.2 reshape.708
  41.8 0.1 compare_reduce_fusion.1
  41.9 0.1 and.518
  42.0 0.1 convert_reduce_fusion.2
  42.1 0.6 fusion.40
  42.7 1.3 %pad_add_fusion.6.count_ref = s32[2]{0:T(128)S(1)} fusion(s32[1]{0:T(128)} %get-tuple-element.313, s32[1]{0:T(128)} %get-tuple-element.312), kind=kLoop, calls=%fused_computation.173 | loop fusion | flops 2 | bytes 16 | tf_op jit(solution)/shard_map/stack | solution.py:233
  44.0 0.4 select_reduce_fusion.12
  44.4 0.1 select_reduce_fusion.13
  44.6 0.7 pack.4
  45.4 2.9 %collective-permute-start.10 = (f32[6,128,128]{2,1,0:T(8,128)S(1)}, f32[6,128,128]{2,1,0:T(8,128)S(1)}, u32[]{:S(2)}, u32[]{:S(2)}) collective-permute-start(f32[6,128,128]{2,1,0:T(8,128)S(1)} %get-tuple-element.193.rest_0_), channel_id=1, source_target_pairs={{32,0},{48,16},{64,32},{80,48},{96,64},{112,80},{0,96},{16,112},{3... | collective-permute-start | bytes 1179656 | tf_op jit(solution)/shard_map/ppermute | solution.py:151
  48.3 0.0 collective-permute-start.9
  48.3 1.4 %collective-permute-start.13 = (f32[6,128,128]{2,1,0:T(8,128)S(1)}, f32[6,128,128]{2,1,0:T(8,128)S(1)}, u32[]{:S(2)}, u32[]{:S(2)}) collective-permute-start(f32[6,128,128]{2,1,0:T(8,128)S(1)} %get-tuple-element.194), channel_id=1, source_target_pairs={{16,0},{0,16},{48,32},{32,48},{80,64},{64,80},{112,96},{96,112},{1... | collective-permute-start | bytes 1179656 | tf_op jit(solution)/shard_map/ppermute | solution.py:235
  49.7 0.2 reshape.721
  49.9 0.1 reshape.709
  50.1 0.7 compare_reduce_fusion.2
  50.9 0.7 convert_reduce_fusion.1
  51.6 0.7 fusion.12
  52.3 0.6 iota_reduce_fusion
  53.0 0.1 add_select_fusion
  53.1 0.8 compare_reduce_fusion
  53.9 6.8 %collective-permute-done.13.rest_5_ = f32[6,128,128]{2,1,0:T(8,128)S(1)} collective-permute-done((f32[6,128,128]{2,1,0:T(8,128)S(1)}, f32[6,128,128]{2,1,0:T(8,128)S(1)}, u32[]{:S(2)}, u32[]{:S(2)}) %collective-permute-start.13) | collective-permute-done | bytes 393248 | tf_op jit(solution)/shard_map/ppermute | solution.py:235
  60.7 3.0 %collective-permute-start.15 = (f32[6,128,128]{2,1,0:T(8,128)S(1)}, f32[6,128,128]{2,1,0:T(8,128)S(1)}, u32[]{:S(2)}, u32[]{:S(2)}) collective-permute-start(f32[6,128,128]{2,1,0:T(8,128)S(1)} %collective-permute-done.13.rest_5_), channel_id=1, source_target_pairs={{32,0},{48,16},{64,32},{80,48},{96,64},{112,80},{0,96},{16,112},{3... | collective-permute-start | bytes 1179656 | tf_op jit(solution)/shard_map/ppermute | solution.py:151
  63.7 0.0 collective-permute-start.14
  63.7 0.1 reshape.712
  63.8 0.6 reduce_sum.199
  64.5 0.7 reduce_max.9
  65.8 0.2 select_reduce_fusion.11
  66.0 0.0 collective-permute-done.10.rest_2_
  66.0 3.3 %collective-permute-start.12 = (f32[3,128,128]{2,1,0:T(8,128)S(1)}, f32[3,128,128]{2,1,0:T(8,128)S(1)}, u32[]{:S(2)}, u32[]{:S(2)}) collective-permute-start(f32[3,128,128]{2,1,0:T(8,128)S(1)} %slice.104), channel_id=1, source_target_pairs={{32,0},{48,16},{64,32},{80,48},{96,64},{112,80},{0,96},{16,112},{3... | collective-permute-start | bytes 589832 | tf_op jit(solution)/shard_map/ppermute | solution.py:151
  69.3 0.0 collective-permute-done.9.rest_1_
  69.3 0.1 collective-permute-start.11
  69.4 3.9 %collective-permute-done.15.rest_7_ = f32[6,128,128]{2,1,0:T(8,128)S(1)} collective-permute-done((f32[6,128,128]{2,1,0:T(8,128)S(1)}, f32[6,128,128]{2,1,0:T(8,128)S(1)}, u32[]{:S(2)}, u32[]{:S(2)}) %collective-permute-start.15) | collective-permute-done | bytes 393248 | tf_op jit(solution)/shard_map/ppermute | solution.py:151
  73.3 3.8 %collective-permute-start.17 = (f32[3,128,128]{2,1,0:T(8,128)S(1)}, f32[3,128,128]{2,1,0:T(8,128)S(1)}, u32[]{:S(2)}, u32[]{:S(2)}) collective-permute-start(f32[3,128,128]{2,1,0:T(8,128)S(1)} %slice.106), channel_id=1, source_target_pairs={{32,0},{48,16},{64,32},{80,48},{96,64},{112,80},{0,96},{16,112},{3... | collective-permute-start | bytes 589832 | tf_op jit(solution)/shard_map/ppermute | solution.py:151
  77.0 0.0 collective-permute-done.14.rest_6_
  77.0 0.1 collective-permute-start.16
  77.1 0.8 select_reduce_fusion.7
  77.9 0.0 collective-permute-done.12.rest_4_
  77.9 2.8 %collective-permute-done.11.rest_3_ = f32[3,128,128]{2,1,0:T(8,128)S(1)} collective-permute-done((f32[3,128,128]{2,1,0:T(8,128)S(1)}, f32[3,128,128]{2,1,0:T(8,128)S(1)}, u32[]{:S(2)}, u32[]{:S(2)}) %collective-permute-start.11) | collective-permute-done | bytes 196640 | tf_op jit(solution)/shard_map/ppermute | solution.py:151
  80.7 0.0 collective-permute-done.17.rest_9_
  80.7 3.3 %collective-permute-done.16.rest_8_ = f32[3,128,128]{2,1,0:T(8,128)S(1)} collective-permute-done((f32[3,128,128]{2,1,0:T(8,128)S(1)}, f32[3,128,128]{2,1,0:T(8,128)S(1)}, u32[]{:S(2)}, u32[]{:S(2)}) %collective-permute-start.16) | collective-permute-done | bytes 196640 | tf_op jit(solution)/shard_map/ppermute | solution.py:151
  84.0 0.0 all-gather.5.cloned.1.call-done
  84.0 4.5 %products.4 = f32[16,128,128]{2,1,0:T(8,128)} custom-call(s32[512]{0:T(512)S(1)} %get-tuple-element.243.a_at, s32[512]{0:T(512)S(1)} %get-tuple-element.242.b_part, s32[512]{0:T(512)S(1)} %get-tuple-element.241.b_at, s32[512]{0:T(512)S(1)} %get-tuple-element.240.c_at, s32[1]{0:T(128)} %bitcast.18.count_ref, f32[64,128,128]{2,1,0:T(8,128)} %bitcast.112, ...), custom_call_target="tpu_custom_call" | custom-call | tf_op jit(solution)/shard_map/products/pallas_call | solution.py:119
  88.5 0.2 while.13
  (39 shorter events, 0.5 us)
Async XLA Ops:
  6.5 77.5 %all-gather.5.cloned.1.call-start = ((), (), s32[]{:S(2)}) async-start(), calls=%async_computation | async-start | bytes 4456448 | tf_op jit(solution)/shard_map/all_gather | solution.py:174
  45.4 20.6 %collective-permute-start.10 = (f32[6,128,128]{2,1,0:T(8,128)S(1)}, f32[6,128,128]{2,1,0:T(8,128)S(1)}, u32[]{:S(2)}, u32[]{:S(2)}) collective-permute-start(f32[6,128,128]{2,1,0:T(8,128)S(1)} %get-tuple-element.193.rest_0_), channel_id=1, source_target_pairs={{32,0},{48,16},{64,32},{80,48},{96,64},{112,80},{0,96},{16,112},{3... | collective-permute-start | bytes 1179656 | tf_op jit(solution)/shard_map/ppermute | solution.py:151
  48.3 21.0 %collective-permute-start.9 = (f32[6,128,128]{2,1,0:T(8,128)S(1)}, f32[6,128,128]{2,1,0:T(8,128)S(1)}, u32[]{:S(2)}, u32[]{:S(2)}) collective-permute-start(f32[6,128,128]{2,1,0:T(8,128)S(1)} %get-tuple-element.193.rest_0_), channel_id=1, source_target_pairs={{96,0},{112,16},{0,32},{16,48},{32,64},{48,80},{64,96},{80,112},{9... | collective-permute-start | bytes 1179656 | tf_op jit(solution)/shard_map/ppermute | solution.py:151
  48.3 12.5 %collective-permute-start.13 = (f32[6,128,128]{2,1,0:T(8,128)S(1)}, f32[6,128,128]{2,1,0:T(8,128)S(1)}, u32[]{:S(2)}, u32[]{:S(2)}) collective-permute-start(f32[6,128,128]{2,1,0:T(8,128)S(1)} %get-tuple-element.194), channel_id=1, source_target_pairs={{16,0},{0,16},{48,32},{32,48},{80,64},{64,80},{112,96},{96,112},{1... | collective-permute-start | bytes 1179656 | tf_op jit(solution)/shard_map/ppermute | solution.py:235
  60.7 12.5 %collective-permute-start.15 = (f32[6,128,128]{2,1,0:T(8,128)S(1)}, f32[6,128,128]{2,1,0:T(8,128)S(1)}, u32[]{:S(2)}, u32[]{:S(2)}) collective-permute-start(f32[6,128,128]{2,1,0:T(8,128)S(1)} %collective-permute-done.13.rest_5_), channel_id=1, source_target_pairs={{32,0},{48,16},{64,32},{80,48},{96,64},{112,80},{0,96},{16,112},{3... | collective-permute-start | bytes 1179656 | tf_op jit(solution)/shard_map/ppermute | solution.py:151
  63.7 13.4 %collective-permute-start.14 = (f32[6,128,128]{2,1,0:T(8,128)S(1)}, f32[6,128,128]{2,1,0:T(8,128)S(1)}, u32[]{:S(2)}, u32[]{:S(2)}) collective-permute-start(f32[6,128,128]{2,1,0:T(8,128)S(1)} %collective-permute-done.13.rest_5_), channel_id=1, source_target_pairs={{96,0},{112,16},{0,32},{16,48},{32,64},{48,80},{64,96},{80,112},{9... | collective-permute-start | bytes 1179656 | tf_op jit(solution)/shard_map/ppermute | solution.py:151
  66.0 11.9 %collective-permute-start.12 = (f32[3,128,128]{2,1,0:T(8,128)S(1)}, f32[3,128,128]{2,1,0:T(8,128)S(1)}, u32[]{:S(2)}, u32[]{:S(2)}) collective-permute-start(f32[3,128,128]{2,1,0:T(8,128)S(1)} %slice.104), channel_id=1, source_target_pairs={{32,0},{48,16},{64,32},{80,48},{96,64},{112,80},{0,96},{16,112},{3... | collective-permute-start | bytes 589832 | tf_op jit(solution)/shard_map/ppermute | solution.py:151
  69.3 11.4 %collective-permute-start.11 = (f32[3,128,128]{2,1,0:T(8,128)S(1)}, f32[3,128,128]{2,1,0:T(8,128)S(1)}, u32[]{:S(2)}, u32[]{:S(2)}) collective-permute-start(f32[3,128,128]{2,1,0:T(8,128)S(1)} %slice.103), channel_id=1, source_target_pairs={{96,0},{112,16},{0,32},{16,48},{32,64},{48,80},{64,96},{80,112},{9... | collective-permute-start | bytes 589832 | tf_op jit(solution)/shard_map/ppermute | solution.py:151
  73.3 7.4 %collective-permute-start.17 = (f32[3,128,128]{2,1,0:T(8,128)S(1)}, f32[3,128,128]{2,1,0:T(8,128)S(1)}, u32[]{:S(2)}, u32[]{:S(2)}) collective-permute-start(f32[3,128,128]{2,1,0:T(8,128)S(1)} %slice.106), channel_id=1, source_target_pairs={{32,0},{48,16},{64,32},{80,48},{96,64},{112,80},{0,96},{16,112},{3... | collective-permute-start | bytes 589832 | tf_op jit(solution)/shard_map/ppermute | solution.py:151
  77.0 6.9 %collective-permute-start.16 = (f32[3,128,128]{2,1,0:T(8,128)S(1)}, f32[3,128,128]{2,1,0:T(8,128)S(1)}, u32[]{:S(2)}, u32[]{:S(2)}) collective-permute-start(f32[3,128,128]{2,1,0:T(8,128)S(1)} %slice.105), channel_id=1, source_target_pairs={{96,0},{112,16},{0,32},{16,48},{32,64},{48,80},{64,96},{80,112},{9... | collective-permute-start | bytes 589832 | tf_op jit(solution)/shard_map/ppermute | solution.py:151
Sparse Core Ops, SparseCore 0:
  9.1 39.6 all-gather.4
where the time goes:
time: 95.8 us; the launch traced here: 95.5 us
  blocking collectives  32.2 us (34%)
  waiting for transfers between devices  17.5 us (18%)
  starting transfers between devices  14.5 us (15%)
  between operations  14.4 us (15%)
  other arithmetic  8.95 us (9%)
  Pallas kernels  5.22 us (5%)
  local copies, waits for them, and re-layouts  2.57 us (3%)
    all_gather x1, blocking collectives, per_device(): lax.all_gather(mine, ('row', 'col'), tiled=True).reshape(rows, columns, -1)  32.2 us
    ppermute x8, starting transfers between devices, ring(): lax.ppermute(block, 'row', [((i + 2 * step) % rows, i) for i in range(row...  13.1 us
    ppermute x8, waiting for transfers between devices, ring(): lax.ppermute(block, 'row', [((i + 2 * step) % rows, i) for i in range(row...  9.96 us
    ppermute x1, waiting for transfers between devices, one_round(): crossed = lax.ppermute(there, 'row', [(i ^ 1, i) for i in range(rows)])  6.81 us
    pallas_call x1, Pallas kernels, products(): pl.pallas_call(functools.partial(product_kernel, first, len(b_parts)), gr...  4.48 us
  transfers between devices with their start and end apart: 10, of which 4 were waited for; matrix products, arithmetic and copies ran while one was open for 12% of the time, Pallas kernels for 1%

commit v1 on v0

--- a/solution.py
+++ b/solution.py
@@ -157,6 +157,26 @@
     return [block, behind, ahead, *far]
 
 
+def everywhere(mine, rows, columns):
+    me = lax.axis_index("row") * columns + lax.axis_index("col")
+    held = mine
+    for bits in ((5, 6), (3, 4), (1, 2), (0,)):
+        group = jnp.zeros((2 ** len(bits),) + held.shape, held.dtype)
+        for move in range(2 ** len(bits)):
+            flip = sum(((move >> n) & 1) << bit for n, bit in enumerate(bits))
+            got = held
+            if move:
+                got = lax.ppermute(
+                    held, ("row", "col"), [(i ^ flip, i) for i in range(rows * columns)]
+                )
+            spot = sum((((me ^ flip) >> bit) & 1) << n for n, bit in enumerate(bits))
+            group = lax.dynamic_update_index_in_dim(group, got, spot, 0)
+        held = group
+    length = mine.shape[0]
+    held = held.reshape(2, 4, 2, 2, 4, length).transpose(4, 2, 3, 1, 0, 5)
+    return held.reshape(rows, columns, length)
+
+
 def per_device(a_blocks, a_index, b_blocks, b_index, c_index):
     rows = lax.axis_size("row")
     columns = lax.axis_size("col")
@@ -169,8 +189,8 @@
     half = row % 2
 
     mine = jnp.concatenate([a_index[0, 0], b_index[0, 0].reshape(-1), c_index[0, 0]])
-    mine = jnp.pad(mine, (0, 128 - mine.shape[0]))[None]
-    spots = lax.all_gather(mine, ("row", "col"), tiled=True).reshape(rows, columns, -1)
+    mine = jnp.pad(mine, (0, 128 - mine.shape[0]))
+    spots = everywhere(mine, rows, columns)
     a_all = lax.all_gather(a_blocks[0, 0], "col").reshape(columns * sa, size, size)
     a_where = spots[:, :, :sa]
     b_where = spots[:, :, sa : sa + held]

time: 95.8 us -> 92.2 us (0.962)
  the two profiles are of different devices: /device:TPU:4 before, /device:TPU:1 now
where the time goes in v1:
time: 92.2 us; the launch traced here: 91.2 us
  waiting for transfers between devices  29.7 us (32%)
  starting transfers between devices  29.5 us (32%)
  between operations  14.5 us (16%)
  other arithmetic  8.95 us (10%)
  Pallas kernels  5.45 us (6%)
  local copies, waits for them, and re-layouts  2.86 us (3%)
    ppermute x10, starting transfers between devices, everywhere(): lax.ppermute(held, ('row', 'col'), [(i ^ flip, i) for i in range(rows * c...  17.6 us
    ppermute x1, waiting for transfers between devices, one_round(): crossed = lax.ppermute(there, 'row', [(i ^ 1, i) for i in range(rows)])  11.1 us
    ppermute x8, starting transfers between devices, ring(): lax.ppermute(block, 'row', [((i + 2 * step) % rows, i) for i in range(row...  10.2 us
    ppermute x10, waiting for transfers between devices, everywhere(): lax.ppermute(held, ('row', 'col'), [(i ^ flip, i) for i in range(rows * c...  9.65 us
    ppermute x8, waiting for transfers between devices, ring(): lax.ppermute(block, 'row', [((i + 2 * step) % rows, i) for i in range(row...  8.85 us
    pallas_call x1, Pallas kernels, products(): pl.pallas_call(functools.partial(product_kernel, first, len(b_parts)), gr...  3.85 us
  transfers between devices with their start and end apart: 20, of which 12 were waited for; matrix products, arithmetic and copies ran while one was open for 11% of the time, Pallas kernels for 2%

profile of v1, /device:TPU:1, one launch (start us, length us, event | category | flops | bytes accessed | tf_op | source)
XLA Modules:
  0.0 91.2 jit_solution(6322951045815694199)
XLA Ops:
  6.5 0.8 reshape_squeeze.6
  7.3 0.7 pad_add_fusion.5
  8.0 3.8 %collective-permute-start.10 = (s32[128]{0:T(128)S(1)}, s32[128]{0:T(128)S(1)}, u32[]{:S(2)}, u32[]{:S(2)}) collective-permute-start(s32[128]{0:T(128)S(1)} %get-tuple-element.318), channel_id=1, source_target_pairs={{64,0},{65,1},{66,2},{67,3},{68,4},{69,5},{70,6},{71,7},{72,8},{73... | collective-permute-start | bytes 1544 | tf_op jit(solution)/shard_map/ppermute | solution.py:169
  11.8 0.4 collective-permute-start.9
  12.2 0.4 collective-permute-start.11
  12.6 0.0 all-gather.3.cloned.1.call-update
  12.8 0.6 iota_reduce_fusion
  13.5 0.7 collective-permute-done.9
  14.3 1.5 %collective-permute-done.11 = s32[128]{0:T(128)S(1)} collective-permute-done((s32[128]{0:T(128)S(1)}, s32[128]{0:T(128)S(1)}, u32[]{:S(2)}, u32[]{:S(2)}) %collective-permute-start.11) | collective-permute-done | bytes 544 | tf_op jit(solution)/shard_map/ppermute | solution.py:169
  15.8 2.5 %collective-permute-start.14 = (s32[4,128]{1,0:T(4,128)S(1)}, s32[4,128]{1,0:T(4,128)S(1)}, u32[]{:S(2)}, u32[]{:S(2)}) collective-permute-start(s32[4,128]{1,0:T(4,128)S(1)} %dynamic_update_slice.49), channel_id=1, source_target_pairs={{24,0},{25,1},{26,2},{27,3},{28,4},{29,5},{30,6},{31,7},{16,8},{17... | collective-permute-start | bytes 6152 | tf_op jit(solution)/shard_map/ppermute | solution.py:169
  18.4 0.5 collective-permute-start.13
  18.9 0.3 collective-permute-start.12
  19.2 2.2 %collective-permute-done.12 = s32[4,128]{1,0:T(4,128)S(1)} collective-permute-done((s32[4,128]{1,0:T(4,128)S(1)}, s32[4,128]{1,0:T(4,128)S(1)}, u32[]{:S(2)}, u32[]{:S(2)}) %collective-permute-start.12) | collective-permute-done | bytes 2080 | tf_op jit(solution)/shard_map/ppermute | solution.py:169
  21.4 1.0 %collective-permute-done.13 = s32[4,128]{1,0:T(4,128)S(1)} collective-permute-done((s32[4,128]{1,0:T(4,128)S(1)}, s32[4,128]{1,0:T(4,128)S(1)}, u32[]{:S(2)}, u32[]{:S(2)}) %collective-permute-start.13) | collective-permute-done | bytes 2080 | tf_op jit(solution)/shard_map/ppermute | solution.py:169
  22.3 0.0 collective-permute-done.14
  22.4 3.8 %collective-permute-start.17 = (s32[4,4,128]{2,1,0:T(4,128)S(1)}, s32[4,4,128]{2,1,0:T(4,128)S(1)}, u32[]{:S(2)}, u32[]{:S(2)}) collective-permute-start(s32[4,4,128]{2,1,0:T(4,128)S(1)} %constant_dynamic-update-slice_fusion), channel_id=1, source_target_pairs={{6,0},{7,1},{4,2},{5,3},{2,4},{3,5},{0,6},{1,7},{14,8},{15,9},{12,... | collective-permute-start | bytes 24584 | tf_op jit(solution)/shard_map/ppermute | solution.py:169
  26.2 0.0 collective-permute-start.16
  26.2 0.7 collective-permute-start.15
  26.9 2.3 %collective-permute-done.15 = s32[4,4,128]{2,1,0:T(4,128)S(1)} collective-permute-done((s32[4,4,128]{2,1,0:T(4,128)S(1)}, s32[4,4,128]{2,1,0:T(4,128)S(1)}, u32[]{:S(2)}, u32[]{:S(2)}) %collective-permute-start.15) | collective-permute-done | bytes 8224 | tf_op jit(solution)/shard_map/ppermute | solution.py:169
  29.2 1.1 %collective-permute-done.16 = s32[4,4,128]{2,1,0:T(4,128)S(1)} collective-permute-done((s32[4,4,128]{2,1,0:T(4,128)S(1)}, s32[4,4,128]{2,1,0:T(4,128)S(1)}, u32[]{:S(2)}, u32[]{:S(2)}) %collective-permute-start.16) | collective-permute-done | bytes 8224 | tf_op jit(solution)/shard_map/ppermute | solution.py:169
  30.3 5.2 %collective-permute-start.18 = (s32[4,4,4,128]{3,2,1,0:T(4,128)S(1)}, s32[4,4,4,128]{3,2,1,0:T(4,128)S(1)}, u32[]{:S(2)}, u32[]{:S(2)}) collective-permute-start(s32[4,4,4,128]{3,2,1,0:T(4,128)S(1)} %bitcast_dynamic-update-slice_fusion.2), channel_id=1, source_target_pairs={{1,0},{0,1},{3,2},{2,3},{5,4},{4,5},{7,6},{6,7},{9,8},{8,9},{11,10... | collective-permute-start | bytes 98312 | tf_op jit(solution)/shard_map/ppermute | solution.py:169
  35.6 0.8 collective-permute-done.18
  36.4 0.1 copy.24
  36.5 0.1 copy.25
  36.6 0.1 broadcast_in_dim.375
  36.7 0.2 reshape.712
  36.9 0.2 reshape.720
  37.0 0.1 fusion.39
  37.2 0.1 reshape.710
  37.4 0.1 compare_reduce_fusion.1
  37.5 0.1 and.622
  37.6 0.1 convert_reduce_fusion.2
  37.7 0.6 fusion.40
  38.3 1.3 %pad_add_fusion.6.count_ref = s32[2]{0:T(128)S(1)} fusion(s32[1]{0:T(128)} %get-tuple-element.313, s32[1]{0:T(128)} %get-tuple-element.312), kind=kLoop, calls=%fused_computation.183 | loop fusion | flops 2 | bytes 16 | tf_op jit(solution)/shard_map/stack | solution.py:253
  39.6 0.4 select_reduce_fusion.12
  40.0 0.1 select_reduce_fusion.13
  40.2 1.6 %pack.4 = (f32[6,128,128]{2,1,0:T(8,128)S(1)}, f32[6,128,128]{2,1,0:T(8,128)S(1)}) custom-call(s32[2,6]{1,0:T(2,128)S(1)} %pad_add_fusion.4.order_ref, s32[2]{0:T(128)S(1)} %pad_add_fusion.6.count_ref, f32[16,128,128]{2,1,0:T(8,128)} %bitcast.140), custom_call_target="tpu_custom_call" | custom-call | tf_op jit(solution)/shard_map/pack/pallas_call | solution.py:44
  41.8 0.1 collective-permute-start.20
  41.9 1.5 %collective-permute-start.19 = (f32[6,128,128]{2,1,0:T(8,128)S(1)}, f32[6,128,128]{2,1,0:T(8,128)S(1)}, u32[]{:S(2)}, u32[]{:S(2)}) collective-permute-start(f32[6,128,128]{2,1,0:T(8,128)S(1)} %get-tuple-element.193.rest_0_), channel_id=1, source_target_pairs={{96,0},{112,16},{0,32},{16,48},{32,64},{48,80},{64,96},{80,112},{9... | collective-permute-start | bytes 1179656 | tf_op jit(solution)/shard_map/ppermute | solution.py:151
  43.4 0.1 reshape.713
  43.5 1.8 %collective-permute-start.23 = (f32[6,128,128]{2,1,0:T(8,128)S(1)}, f32[6,128,128]{2,1,0:T(8,128)S(1)}, u32[]{:S(2)}, u32[]{:S(2)}) collective-permute-start(f32[6,128,128]{2,1,0:T(8,128)S(1)} %get-tuple-element.194), channel_id=1, source_target_pairs={{16,0},{0,16},{48,32},{32,48},{80,64},{64,80},{112,96},{96,112},{1... | collective-permute-start | bytes 1179656 | tf_op jit(solution)/shard_map/ppermute | solution.py:255
  45.3 0.7 compare_reduce_fusion.2
  46.0 0.7 convert_reduce_fusion.1
  46.7 0.7 fusion.12
  47.6 0.1 add_select_fusion
  47.7 0.8 compare_reduce_fusion
  48.5 11.1 %collective-permute-done.23.rest_5_ = f32[6,128,128]{2,1,0:T(8,128)S(1)} collective-permute-done((f32[6,128,128]{2,1,0:T(8,128)S(1)}, f32[6,128,128]{2,1,0:T(8,128)S(1)}, u32[]{:S(2)}, u32[]{:S(2)}) %collective-permute-start.23) | collective-permute-done | bytes 393248 | tf_op jit(solution)/shard_map/ppermute | solution.py:255
  59.6 2.3 %collective-permute-start.25 = (f32[6,128,128]{2,1,0:T(8,128)S(1)}, f32[6,128,128]{2,1,0:T(8,128)S(1)}, u32[]{:S(2)}, u32[]{:S(2)}) collective-permute-start(f32[6,128,128]{2,1,0:T(8,128)S(1)} %collective-permute-done.23.rest_5_), channel_id=1, source_target_pairs={{32,0},{48,16},{64,32},{80,48},{96,64},{112,80},{0,96},{16,112},{3... | collective-permute-start | bytes 1179656 | tf_op jit(solution)/shard_map/ppermute | solution.py:151
  61.9 0.0 collective-permute-start.24
  61.9 0.1 reshape.716
  62.0 0.6 reduce_sum.199
  62.7 0.7 reduce_max.9
  64.0 0.2 select_reduce_fusion.11
  64.2 2.7 %collective-permute-start.22 = (f32[3,128,128]{2,1,0:T(8,128)S(1)}, f32[3,128,128]{2,1,0:T(8,128)S(1)}, u32[]{:S(2)}, u32[]{:S(2)}) collective-permute-start(f32[3,128,128]{2,1,0:T(8,128)S(1)} %slice.104), channel_id=1, source_target_pairs={{32,0},{48,16},{64,32},{80,48},{96,64},{112,80},{0,96},{16,112},{3... | collective-permute-start | bytes 589832 | tf_op jit(solution)/shard_map/ppermute | solution.py:151
  66.9 0.1 collective-permute-start.21
  67.0 2.6 %collective-permute-done.25.rest_7_ = f32[6,128,128]{2,1,0:T(8,128)S(1)} collective-permute-done((f32[6,128,128]{2,1,0:T(8,128)S(1)}, f32[6,128,128]{2,1,0:T(8,128)S(1)}, u32[]{:S(2)}, u32[]{:S(2)}) %collective-permute-start.25) | collective-permute-done | bytes 393248 | tf_op jit(solution)/shard_map/ppermute | solution.py:151
  69.7 3.5 %collective-permute-start.27 = (f32[3,128,128]{2,1,0:T(8,128)S(1)}, f32[3,128,128]{2,1,0:T(8,128)S(1)}, u32[]{:S(2)}, u32[]{:S(2)}) collective-permute-start(f32[3,128,128]{2,1,0:T(8,128)S(1)} %slice.106), channel_id=1, source_target_pairs={{32,0},{48,16},{64,32},{80,48},{96,64},{112,80},{0,96},{16,112},{3... | collective-permute-start | bytes 589832 | tf_op jit(solution)/shard_map/ppermute | solution.py:151
  73.2 0.1 collective-permute-start.26
  73.3 0.8 select_reduce_fusion.7
  74.0 2.9 %collective-permute-done.21.rest_3_ = f32[3,128,128]{2,1,0:T(8,128)S(1)} collective-permute-done((f32[3,128,128]{2,1,0:T(8,128)S(1)}, f32[3,128,128]{2,1,0:T(8,128)S(1)}, u32[]{:S(2)}, u32[]{:S(2)}) %collective-permute-start.21) | collective-permute-done | bytes 196640 | tf_op jit(solution)/shard_map/ppermute | solution.py:151
  77.0 0.9 collective-permute-done.27.rest_9_
  77.9 2.4 %collective-permute-done.26.rest_8_ = f32[3,128,128]{2,1,0:T(8,128)S(1)} collective-permute-done((f32[3,128,128]{2,1,0:T(8,128)S(1)}, f32[3,128,128]{2,1,0:T(8,128)S(1)}, u32[]{:S(2)}, u32[]{:S(2)}) %collective-permute-start.26) | collective-permute-done | bytes 196640 | tf_op jit(solution)/shard_map/ppermute | solution.py:151
  80.2 3.9 %products.4 = f32[16,128,128]{2,1,0:T(8,128)} custom-call(s32[512]{0:T(512)S(1)} %get-tuple-element.243.a_at, s32[512]{0:T(512)S(1)} %get-tuple-element.242.b_part, s32[512]{0:T(512)S(1)} %get-tuple-element.241.b_at, s32[512]{0:T(512)S(1)} %get-tuple-element.240.c_at, s32[1]{0:T(128)} %bitcast.33.count_ref, f32[64,128,128]{2,1,0:T(8,128)} %bitcast.138, ...), custom_call_target="tpu_custom_call" | custom-call | tf_op jit(solution)/shard_map/products/pallas_call | solution.py:119
  84.1 0.2 while.13
  (65 shorter events, 0.7 us)
Async XLA Ops:
  6.5 73.7 %all-gather.3.cloned.1.call-start = ((), (), s32[]{:S(2)}) async-start(), calls=%async_computation | async-start | bytes 4456448 | tf_op jit(solution)/shard_map/all_gather | solution.py:194
  8.0 6.2 %collective-permute-start.10 = (s32[128]{0:T(128)S(1)}, s32[128]{0:T(128)S(1)}, u32[]{:S(2)}, u32[]{:S(2)}) collective-permute-start(s32[128]{0:T(128)S(1)} %get-tuple-element.318), channel_id=1, source_target_pairs={{64,0},{65,1},{66,2},{67,3},{68,4},{69,5},{70,6},{71,7},{72,8},{73... | collective-permute-start | bytes 1544 | tf_op jit(solution)/shard_map/ppermute | solution.py:169
  11.8 2.4 %collective-permute-start.9 = (s32[128]{0:T(128)S(1)}, s32[128]{0:T(128)S(1)}, u32[]{:S(2)}, u32[]{:S(2)}) collective-permute-start(s32[128]{0:T(128)S(1)} %get-tuple-element.318), channel_id=1, source_target_pairs={{32,0},{33,1},{34,2},{35,3},{36,4},{37,5},{38,6},{39,7},{40,8},{41... | collective-permute-start | bytes 1544 | tf_op jit(solution)/shard_map/ppermute | solution.py:169
  12.2 3.6 %collective-permute-start.11 = (s32[128]{0:T(128)S(1)}, s32[128]{0:T(128)S(1)}, u32[]{:S(2)}, u32[]{:S(2)}) collective-permute-start(s32[128]{0:T(128)S(1)} %get-tuple-element.318), channel_id=1, source_target_pairs={{96,0},{97,1},{98,2},{99,3},{100,4},{101,5},{102,6},{103,7},{104,8... | collective-permute-start | bytes 1544 | tf_op jit(solution)/shard_map/ppermute | solution.py:169
  15.8 6.5 %collective-permute-start.14 = (s32[4,128]{1,0:T(4,128)S(1)}, s32[4,128]{1,0:T(4,128)S(1)}, u32[]{:S(2)}, u32[]{:S(2)}) collective-permute-start(s32[4,128]{1,0:T(4,128)S(1)} %dynamic_update_slice.49), channel_id=1, source_target_pairs={{24,0},{25,1},{26,2},{27,3},{28,4},{29,5},{30,6},{31,7},{16,8},{17... | collective-permute-start | bytes 6152 | tf_op jit(solution)/shard_map/ppermute | solution.py:169
  18.4 3.9 %collective-permute-start.13 = (s32[4,128]{1,0:T(4,128)S(1)}, s32[4,128]{1,0:T(4,128)S(1)}, u32[]{:S(2)}, u32[]{:S(2)}) collective-permute-start(s32[4,128]{1,0:T(4,128)S(1)} %dynamic_update_slice.49), channel_id=1, source_target_pairs={{16,0},{17,1},{18,2},{19,3},{20,4},{21,5},{22,6},{23,7},{24,8},{25... | collective-permute-start | bytes 6152 | tf_op jit(solution)/shard_map/ppermute | solution.py:169
  18.9 2.4 %collective-permute-start.12 = (s32[4,128]{1,0:T(4,128)S(1)}, s32[4,128]{1,0:T(4,128)S(1)}, u32[]{:S(2)}, u32[]{:S(2)}) collective-permute-start(s32[4,128]{1,0:T(4,128)S(1)} %dynamic_update_slice.49), channel_id=1, source_target_pairs={{8,0},{9,1},{10,2},{11,3},{12,4},{13,5},{14,6},{15,7},{0,8},{1,9},... | collective-permute-start | bytes 6152 | tf_op jit(solution)/shard_map/ppermute | solution.py:169
  22.4 7.9 %collective-permute-start.17 = (s32[4,4,128]{2,1,0:T(4,128)S(1)}, s32[4,4,128]{2,1,0:T(4,128)S(1)}, u32[]{:S(2)}, u32[]{:S(2)}) collective-permute-start(s32[4,4,128]{2,1,0:T(4,128)S(1)} %constant_dynamic-update-slice_fusion), channel_id=1, source_target_pairs={{6,0},{7,1},{4,2},{5,3},{2,4},{3,5},{0,6},{1,7},{14,8},{15,9},{12,... | collective-permute-start | bytes 24584 | tf_op jit(solution)/shard_map/ppermute | solution.py:169
  26.2 4.1 %collective-permute-start.16 = (s32[4,4,128]{2,1,0:T(4,128)S(1)}, s32[4,4,128]{2,1,0:T(4,128)S(1)}, u32[]{:S(2)}, u32[]{:S(2)}) collective-permute-start(s32[4,4,128]{2,1,0:T(4,128)S(1)} %constant_dynamic-update-slice_fusion), channel_id=1, source_target_pairs={{4,0},{5,1},{6,2},{7,3},{0,4},{1,5},{2,6},{3,7},{12,8},{13,9},{14,... | collective-permute-start | bytes 24584 | tf_op jit(solution)/shard_map/ppermute | solution.py:169
  26.2 3.0 %collective-permute-start.15 = (s32[4,4,128]{2,1,0:T(4,128)S(1)}, s32[4,4,128]{2,1,0:T(4,128)S(1)}, u32[]{:S(2)}, u32[]{:S(2)}) collective-permute-start(s32[4,4,128]{2,1,0:T(4,128)S(1)} %constant_dynamic-update-slice_fusion), channel_id=1, source_target_pairs={{2,0},{3,1},{0,2},{1,3},{6,4},{7,5},{4,6},{5,7},{10,8},{11,9},{8,1... | collective-permute-start | bytes 24584 | tf_op jit(solution)/shard_map/ppermute | solution.py:169
  30.3 6.1 %collective-permute-start.18 = (s32[4,4,4,128]{3,2,1,0:T(4,128)S(1)}, s32[4,4,4,128]{3,2,1,0:T(4,128)S(1)}, u32[]{:S(2)}, u32[]{:S(2)}) collective-permute-start(s32[4,4,4,128]{3,2,1,0:T(4,128)S(1)} %bitcast_dynamic-update-slice_fusion.2), channel_id=1, source_target_pairs={{1,0},{0,1},{3,2},{2,3},{5,4},{4,5},{7,6},{6,7},{9,8},{8,9},{11,10... | collective-permute-start | bytes 98312 | tf_op jit(solution)/shard_map/ppermute | solution.py:169
  41.8 22.4 %collective-permute-start.20 = (f32[6,128,128]{2,1,0:T(8,128)S(1)}, f32[6,128,128]{2,1,0:T(8,128)S(1)}, u32[]{:S(2)}, u32[]{:S(2)}) collective-permute-start(f32[6,128,128]{2,1,0:T(8,128)S(1)} %get-tuple-element.193.rest_0_), channel_id=1, source_target_pairs={{32,0},{48,16},{64,32},{80,48},{96,64},{112,80},{0,96},{16,112},{3... | collective-permute-start | bytes 1179656 | tf_op jit(solution)/shard_map/ppermute | solution.py:151
  41.9 25.0 %collective-permute-start.19 = (f32[6,128,128]{2,1,0:T(8,128)S(1)}, f32[6,128,128]{2,1,0:T(8,128)S(1)}, u32[]{:S(2)}, u32[]{:S(2)}) collective-permute-start(f32[6,128,128]{2,1,0:T(8,128)S(1)} %get-tuple-element.193.rest_0_), channel_id=1, source_target_pairs={{96,0},{112,16},{0,32},{16,48},{32,64},{48,80},{64,96},{80,112},{9... | collective-permute-start | bytes 1179656 | tf_op jit(solution)/shard_map/ppermute | solution.py:151
  43.5 16.1 %collective-permute-start.23 = (f32[6,128,128]{2,1,0:T(8,128)S(1)}, f32[6,128,128]{2,1,0:T(8,128)S(1)}, u32[]{:S(2)}, u32[]{:S(2)}) collective-permute-start(f32[6,128,128]{2,1,0:T(8,128)S(1)} %get-tuple-element.194), channel_id=1, source_target_pairs={{16,0},{0,16},{48,32},{32,48},{80,64},{64,80},{112,96},{96,112},{1... | collective-permute-start | bytes 1179656 | tf_op jit(solution)/shard_map/ppermute | solution.py:255
  59.6 10.1 %collective-permute-start.25 = (f32[6,128,128]{2,1,0:T(8,128)S(1)}, f32[6,128,128]{2,1,0:T(8,128)S(1)}, u32[]{:S(2)}, u32[]{:S(2)}) collective-permute-start(f32[6,128,128]{2,1,0:T(8,128)S(1)} %collective-permute-done.23.rest_5_), channel_id=1, source_target_pairs={{32,0},{48,16},{64,32},{80,48},{96,64},{112,80},{0,96},{16,112},{3... | collective-permute-start | bytes 1179656 | tf_op jit(solution)/shard_map/ppermute | solution.py:151
  61.9 11.3 %collective-permute-start.24 = (f32[6,128,128]{2,1,0:T(8,128)S(1)}, f32[6,128,128]{2,1,0:T(8,128)S(1)}, u32[]{:S(2)}, u32[]{:S(2)}) collective-permute-start(f32[6,128,128]{2,1,0:T(8,128)S(1)} %collective-permute-done.23.rest_5_), channel_id=1, source_target_pairs={{96,0},{112,16},{0,32},{16,48},{32,64},{48,80},{64,96},{80,112},{9... | collective-permute-start | bytes 1179656 | tf_op jit(solution)/shard_map/ppermute | solution.py:151
  64.2 9.9 %collective-permute-start.22 = (f32[3,128,128]{2,1,0:T(8,128)S(1)}, f32[3,128,128]{2,1,0:T(8,128)S(1)}, u32[]{:S(2)}, u32[]{:S(2)}) collective-permute-start(f32[3,128,128]{2,1,0:T(8,128)S(1)} %slice.104), channel_id=1, source_target_pairs={{32,0},{48,16},{64,32},{80,48},{96,64},{112,80},{0,96},{16,112},{3... | collective-permute-start | bytes 589832 | tf_op jit(solution)/shard_map/ppermute | solution.py:151
  66.9 10.0 %collective-permute-start.21 = (f32[3,128,128]{2,1,0:T(8,128)S(1)}, f32[3,128,128]{2,1,0:T(8,128)S(1)}, u32[]{:S(2)}, u32[]{:S(2)}) collective-permute-start(f32[3,128,128]{2,1,0:T(8,128)S(1)} %slice.103), channel_id=1, source_target_pairs={{96,0},{112,16},{0,32},{16,48},{32,64},{48,80},{64,96},{80,112},{9... | collective-permute-start | bytes 589832 | tf_op jit(solution)/shard_map/ppermute | solution.py:151
  69.7 8.2 %collective-permute-start.27 = (f32[3,128,128]{2,1,0:T(8,128)S(1)}, f32[3,128,128]{2,1,0:T(8,128)S(1)}, u32[]{:S(2)}, u32[]{:S(2)}) collective-permute-start(f32[3,128,128]{2,1,0:T(8,128)S(1)} %slice.106), channel_id=1, source_target_pairs={{32,0},{48,16},{64,32},{80,48},{96,64},{112,80},{0,96},{16,112},{3... | collective-permute-start | bytes 589832 | tf_op jit(solution)/shard_map/ppermute | solution.py:151
  73.2 7.1 %collective-permute-start.26 = (f32[3,128,128]{2,1,0:T(8,128)S(1)}, f32[3,128,128]{2,1,0:T(8,128)S(1)}, u32[]{:S(2)}, u32[]{:S(2)}) collective-permute-start(f32[3,128,128]{2,1,0:T(8,128)S(1)} %slice.105), channel_id=1, source_target_pairs={{96,0},{112,16},{0,32},{16,48},{32,64},{48,80},{64,96},{80,112},{9... | collective-permute-start | bytes 589832 | tf_op jit(solution)/shard_map/ppermute | solution.py:151
Sparse Core Ops, SparseCore 0:
  12.7 44.4 all-gather.2
